TPU v7x, 32 devices: a whole 2x2x4 slice. The times are simulated.
32 devices in a mesh: src: 16 (over z, y, x), inst: 2 (over core).
Axes of the slice: x: 2, y: 2, z: 4, core: 2. Of those that a mesh axis runs over, the one named last changes fastest.
Arguments:
- observed: float32 [60, 16384], P(None, ('src', 'inst')), may hold values from -18 to 18
- basis: float32 [60, 55], replicated, may hold values from -0.875 to 0.875
- taps: float32 [9], replicated, may hold values from 0.05 to 0.35
- epoch_owner: int32 [16384, 1], P(('src', 'inst')), may hold values from 0 to 15; in each aligned block of 512 rows (0 to 511, 512 to 1023, ...) at most 48 rows name the same one
- epoch_source: int32 [16384], P(('src', 'inst')), may hold values from 0 to 4095
- epoch_config: int32 [16384], P(('src', 'inst')), may hold values from 0 to 31
- epoch_counts: int32 [32], P(('src', 'inst')), may hold values from 256 to 512, as said below
Outputs:
- solution_coeffs: float32 [55, 65536], P(None, 'src')
- solution_table: float32 [60, 32], P(None, 'inst')
- direction_coeffs: float32 [55, 65536], P(None, 'src')
- direction_table: float32 [60, 32], P(None, 'inst')
Inputs may be any that keep to these rules, and one draw needn't show every extreme that they name: `epoch_owner`: among the 512 epochs of one device, at most 48 name any one owner. The first epoch_counts[d] of device d's 512 epoch slots are live.
All inputs are finite; a program needn't handle non-finite values.
Results may differ from a plain program's by a relative error of at most 0.0003.
Values sent between devices are 32-bit elements; how exact they have to be, the bound alone decides.
A program may use at most 64 MiB of HBM per device.

v0:
```python
import functools

import jax
import jax.numpy as jnp
from jax import lax
from jax.experimental import pallas as pl
from jax.experimental.pallas import tpu as pltpu
from jax.sharding import PartitionSpec as P

SRC_DEV = 4096
KDEV = 16
F = 64
MESH = pl.DeviceIdType.MESH
HIGHEST = lax.Precision.HIGHEST
f32, bf16 = jnp.float32, jnp.bfloat16


def iota(shape, dim):
    return lax.broadcasted_iota(jnp.int32, shape, dim)


def pieces(x, count):
    out = []
    for _ in range(count - 1):
        head = x.astype(bf16)
        out.append(head)
        x = x - head.astype(f32)
    out.append(x.astype(bf16))
    return out


def dot3(a, b):
    ah, al = pieces(a, 2)
    bh, bl = pieces(b, 2)
    return jnp.dot(
        jnp.concatenate([ah, al, ah], 1),
        jnp.concatenate([bh, bh, bl], 0),
        preferred_element_type=f32,
    )


def exact(a, b, dims=(((1,), (0,)), ((), ()))):
    return lax.dot_general(a, b, dims, precision=HIGHEST, preferred_element_type=f32)


def fold(onehot, x):
    width = x.shape[1]
    got = lax.dot_general(
        onehot, jnp.concatenate(pieces(x, 3), 1), (((0,), (0,)), ((), ())), preferred_element_type=f32
    )
    return got[:, :width] + got[:, width : 2 * width] + got[:, 2 * width :]


def total(x):
    return jnp.sum(x, axis=(0, 1), keepdims=True)


def stack8(x):
    return jnp.sum(x.reshape(x.shape[0] // 8, 8, x.shape[1]), axis=0)


def with_scalars(block, first, *values):
    lane, row = iota(block.shape, 1), iota(block.shape, 0)
    for at, value in enumerate(values):
        block = jnp.where((lane == first + at) & (row == 0), value, block)
    return block


def lanczos(
    dims,
    obs, basis_t, taps, owner, source, config, counts,
    v1_out, v2_out, v3_out, mix_out, xh_out, wh_out,
    send, recv, slots, quads, c0s, cgs, nss, rpad, tables,
    match, zt, cols1, cols2, cols3, grams, counts_c, named_c, out_sem,
    a1, a2, b1, b2, norms,
    send_sem, recv_sem, fsend_sem, frecv_sem, xsend, xrecv, ysend, yrecv, nsend, nrecv,
):
    n_src, n_inst, rows, configs, hi_n, lo_n, chunk, sources = dims
    me, mine = lax.axis_index("src"), lax.axis_index("inst")
    my_hi, my_lo = me // lo_n, lax.rem(me, lo_n)
    samples, epochs = obs.shape
    coefs = basis_t.shape[0]
    half_rows = n_inst * n_src * rows
    steps = 2 * half_rows // chunk

    barrier = pltpu.get_barrier_semaphore()
    for step in range(1, n_src):
        pl.semaphore_signal(barrier, inc=1, device_id=(lax.rem(me + step, n_src), mine), device_id_type=MESH)
    for step in range(1, n_inst):
        pl.semaphore_signal(barrier, inc=1, device_id=(me, lax.rem(mine + step, n_inst)), device_id_type=MESH)

    own = owner[...]
    table = own == iota((n_src, epochs), 0)
    before = (iota((epochs, epochs), 0) < iota((epochs, epochs), 1)).astype(bf16)
    earlier = jnp.dot(table.astype(bf16), before, preferred_element_type=f32)
    slot = jnp.sum(jnp.where(table, earlier, 0.0), axis=0, keepdims=True).astype(jnp.int32)
    live = iota((1, epochs), 1) < counts[...]
    upper = slot >= rows
    place = jnp.where(live, own * rows + slot - jnp.where(upper, rows, 0), -1)
    hit = place == iota((n_src * rows, epochs), 0)
    data = jnp.concatenate(
        [
            obs[...],
            (source[...] + 1).astype(f32),
            config[...].astype(f32),
            jnp.ones((1, epochs), f32),
            jnp.zeros((F - samples - 3, epochs), f32),
        ],
        0,
    )
    stacked = jnp.concatenate(pieces(data, 3), 0)

    def packed(mask):
        got = lax.dot_general(
            mask.astype(bf16), stacked, (((1,), (1,)), ((), ())), preferred_element_type=f32
        )
        return got[:, :F] + got[:, F : 2 * F] + got[:, 2 * F :]

    send[...] = jnp.concatenate([packed(hit & ~upper), packed(hit & upper)], 1).reshape(n_src, rows, 2 * F)
    recv[mine, me] = send[me]

    pl.semaphore_wait(barrier, n_src + n_inst - 2)
    for step in range(1, n_src):
        peer = lax.rem(me + step, n_src)
        pltpu.make_async_remote_copy(
            send.at[peer], recv.at[mine, me], send_sem.at[peer], recv_sem.at[me],
            device_id=(peer, mine), device_id_type=MESH,
        ).start()

    spread = jnp.zeros((samples, samples), f32)
    offset = iota((samples, samples), 1) - iota((samples, samples), 0) + taps.shape[0] // 2
    for tap in range(taps.shape[0]):
        spread = jnp.where(offset == tap, taps[tap], spread)
    rpad[...] = jnp.zeros((F, F), f32)
    rpad[pl.ds(0, samples), pl.ds(0, coefs)] = exact(spread, basis_t[...], (((1,), (1,)), ((), ())))
    resp = rpad[...]
    gram = exact(resp, resp, (((0,), (0,)), ((), ())))
    resp_t = resp.T
    cweight = 0.4 * (1.0 + 3.0 * iota((configs, 1), 0).astype(f32) / configs)

    for step in range(1, n_src):
        peer = lax.rem(me + step, n_src)
        pltpu.make_async_remote_copy(
            send.at[peer], recv.at[mine, peer], send_sem.at[peer], recv_sem.at[peer],
            device_id=(peer, mine), device_id_type=MESH,
        ).wait()
    forwards = []
    for step in range(1, n_inst):
        other = lax.rem(mine + step, n_inst)
        pltpu.make_async_remote_copy(
            recv.at[mine], recv.at[mine], fsend_sem.at[other], frecv_sem.at[mine],
            device_id=(me, other), device_id_type=MESH,
        ).start()
        forwards.append(
            pltpu.make_async_remote_copy(
                recv.at[mine], recv.at[other], fsend_sem.at[other], frecv_sem.at[other],
                device_id=(me, other), device_id_type=MESH,
            )
        )
    for forward in forwards:
        forward.wait()

    held = recv[...].reshape(half_rows, 2 * F)
    slots[pl.ds(0, half_rows), :] = held[:, :F]
    slots[pl.ds(half_rows, half_rows), :] = held[:, F:]
    pick = (iota((8, 2 * F), 1) == samples + F * iota((8, 2 * F), 0)).astype(bf16)
    names = sum(
        lax.dot_general(pick, piece, (((1,), (1,)), ((), ())), preferred_element_type=f32)
        for piece in pieces(held, 2)
    )
    id_row = jnp.concatenate([names[0:1], names[1:2]], 1)
    id_row = jnp.where(id_row > 0.5, id_row, -1.0)
    lane = iota((1, F), 1)

    def at(step):
        return pl.ds(pl.multiple_of(step * chunk, chunk), chunk)

    def config_table(part):
        return (
            (part[:, samples + 1 : samples + 2] == iota((chunk, configs), 1).astype(f32))
            & (part[:, samples + 2 : samples + 3] > 0.5)
        ).astype(bf16)

    def project(step, carry):
        part = slots[at(step), :]
        spectra = jnp.where(lane < samples, part, 0.0)
        quads[at(step), :] = jnp.concatenate(
            pieces(dot3(spectra, resp), 2)
            + [jnp.broadcast_to(part[:, samples + 2 : samples + 3], (chunk, F)).astype(bf16), config_table(part)],
            1,
        )
        return carry + stack8(spectra * spectra)

    none = jnp.zeros((8, F), f32)
    unroll = steps <= 4
    b_sq = total(lax.fori_loop(0, steps, project, none, unroll=unroll))

    def gather(step, carry):
        stats, c_sq, quad = carry
        part = slots[at(step), :]
        name = part[:, samples : samples + 1]
        same = jnp.where(name == id_row, 1.0, 0.0).astype(bf16)
        got = jnp.dot(same, quads[...], preferred_element_type=f32)
        c0 = got[:, :F] + got[:, F : 2 * F]
        count = got[:, 2 * F : 3 * F]
        weight = 1.0 / jnp.maximum(count, 1.0)
        cg = dot3(c0, gram)
        c0s[at(step), :] = c0
        cgs[at(step), :] = count * cg
        nss[at(step), :] = got[:, 3 * F :]
        stats = stats + fold(config_table(part), jnp.concatenate([part, c0], 1))
        return stats, c_sq + stack8(c0 * c0 * weight), quad + stack8(c0 * cg)

    stats, c_sq, quad = lax.fori_loop(
        0, steps, gather, (jnp.zeros((configs, 2 * F), f32), none, none), unroll=unroll
    )

    lanes = match.shape[1]
    block = 512

    def here(at_block):
        return slice(None), pl.ds(pl.multiple_of(at_block * block, block), block)

    def deposit(at_block, carry):
        hit = jnp.concatenate(
            [
                jnp.where(
                    match[...] == (at_block * (block // lanes) + i).astype(f32).astype(bf16), 1.0, 0.0
                ).astype(bf16)
                for i in range(block // lanes)
            ],
            1,
        )
        got = jnp.dot(zt[...], hit, preferred_element_type=f32)
        c0 = got[:F] + got[F : 2 * F]
        cols1[here(at_block)] = c0
        counts_c[here(at_block)] = got[2 * F : 3 * F]
        named_c[here(at_block)] = got[3 * F :]
        grams[here(at_block)] = got[2 * F : 3 * F] * dot3(gram, c0)
        return carry

    def emit(which, cols, out):
        return pltpu.make_async_copy(cols, out, out_sem.at[which])

    blocks = sources // block

    def prepare_first():
        name = slots[:, samples : samples + 1].astype(jnp.int32) - 1
        match[...] = jnp.where((name & (lanes - 1)) == iota(match.shape, 1), name // lanes, -1).astype(f32).astype(bf16)
        zt[...] = quads[...].astype(f32).T.astype(bf16)
        lax.fori_loop(0, blocks // 4, deposit, 0)

    def finish_first():
        lax.fori_loop(blocks // 4, blocks, deposit, 0)

    def second_columns(first, last):
        hr1_t = hr1.T

        def one_block(at_block, carry):
            v2 = (grams[here(at_block)] - diag1 * cols1[here(at_block)]) * inv_p + dot3(hr1_t, named_c[here(at_block)])
            cols2[here(at_block)] = v2
            grams[here(at_block)] = counts_c[here(at_block)] * dot3(gram, v2)
            return carry

        lax.fori_loop(first, last, one_block, 0)

    def swap(which, value, one_buf, two_buf, work1, work2):
        one_buf[my_hi] = value
        sent = []
        for step in range(1, hi_n):
            peer = lax.rem(my_hi + step, hi_n)
            pltpu.make_async_remote_copy(
                one_buf.at[my_hi], one_buf.at[my_hi], xsend.at[which, peer], xrecv.at[which, my_hi],
                device_id=(peer * lo_n + my_lo, mine), device_id_type=MESH,
            ).start()
            sent.append(pltpu.make_async_remote_copy(
                one_buf.at[my_hi], one_buf.at[peer], xsend.at[which, peer], xrecv.at[which, peer],
                device_id=(peer * lo_n + my_lo, mine), device_id_type=MESH,
            ))
        work1()
        for copy in sent:
            copy.wait()
        two_buf[my_lo] = jnp.sum(one_buf[...], axis=0)
        sent = []
        for step in range(1, lo_n):
            peer = lax.rem(my_lo + step, lo_n)
            pltpu.make_async_remote_copy(
                two_buf.at[my_lo], two_buf.at[my_lo], ysend.at[which, peer], yrecv.at[which, my_lo],
                device_id=(my_hi * lo_n + peer, mine), device_id_type=MESH,
            ).start()
            sent.append(pltpu.make_async_remote_copy(
                two_buf.at[my_lo], two_buf.at[peer], ysend.at[which, peer], yrecv.at[which, peer],
                device_id=(my_hi * lo_n + peer, mine), device_id_type=MESH,
            ))
        work2()
        for copy in sent:
            copy.wait()
        return jnp.sum(two_buf[...], axis=0)

    spare = 2 * F - 4
    got = swap(0, with_scalars(stats, spare, b_sq, total(c_sq), total(quad)), a1, a2,
               prepare_first, finish_first)
    emit(0, cols1, v1_out).start()
    b_sq, c_sq, quad = [got[0:1, spare + i : spare + i + 1] for i in range(3)]
    per_config = got[:configs, samples + 2 : samples + 3]
    h0 = jnp.where(lane < samples, got[:configs, :F], 0.0) * cweight
    p_sq = c_sq + total(h0 * h0)
    inv_p = 1.0 / jnp.sqrt(p_sq)
    beta1 = jnp.sqrt(b_sq)
    alpha1 = jnp.sqrt(p_sq) / beta1

    def table_step(h, s):
        hr = dot3(cweight * h, resp)
        mh = cweight * (dot3(s, resp_t) + per_config * cweight * h)
        return hr, mh, total(hr * s) + total(h * mh)

    h1 = h0 * inv_p
    hr1, mh1, extra = table_step(h1, jnp.where(lane < coefs, got[:, F:], 0.0) * inv_p)
    diag1 = quad * inv_p * inv_p + extra
    beta2 = jnp.sqrt(diag1 - alpha1 * alpha1)

    def second(step, carry):
        stats, v_sq, quad = carry
        named = nss[at(step), :]
        weight = 1.0 / jnp.maximum(jnp.sum(named, axis=1, keepdims=True), 1.0)
        v2 = (cgs[at(step), :] - diag1 * c0s[at(step), :]) * inv_p + dot3(named, hr1)
        vg = dot3(v2, gram)
        stats = stats + fold(quads[at(step), 3 * F :], v2)
        return stats, v_sq + stack8(v2 * v2 * weight), quad + stack8(v2 * vg)

    stats, v_sq, quad = lax.fori_loop(
        0, steps, second, (jnp.zeros((configs, F), f32), none, none), unroll=unroll
    )
    wide = jnp.concatenate([stats[: configs // 2], stats[configs // 2 :]], 1)
    got = swap(1, with_scalars(wide, spare, total(v_sq), total(quad)), b1, b2,
               lambda: second_columns(0, blocks // 2), lambda: second_columns(blocks // 2, blocks))
    emit(1, cols2, v2_out).start()
    v_sq, quad = [got[0:1, spare + i : spare + i + 1] for i in range(2)]
    h2 = mh1 - diag1 * h1
    off_sq = v_sq + total(h2 * h2)
    off1 = jnp.sqrt(off_sq)
    inv1 = 1.0 / off1
    h2 = h2 * inv1
    s2 = jnp.where(lane < coefs, jnp.concatenate([got[:, :F], got[:, F:]], 0), 0.0) * inv1
    hr2, mh2, extra = table_step(h2, s2)
    diag2 = quad * inv1 * inv1 + extra
    alpha2 = off1 / beta2
    beta3 = jnp.sqrt(diag2 - alpha2 * alpha2)

    hr2_t = hr2.T

    def third(at_block, v_sq):
        v3 = (
            (grams[here(at_block)] - diag2 * cols2[here(at_block)]) * inv1
            - (off1 * inv_p) * cols1[here(at_block)]
            + dot3(hr2_t, named_c[here(at_block)])
        )
        cols3[here(at_block)] = v3
        square = stack8(v3 * v3)
        return v_sq + sum(square[:, i * lanes : (i + 1) * lanes] for i in range(block // lanes))

    v_sq = lax.fori_loop(0, blocks, third, jnp.zeros((8, lanes), f32))
    norms[me] = v_sq
    sent = []
    for step in range(1, n_src):
        peer = lax.rem(me + step, n_src)
        pltpu.make_async_remote_copy(
            norms.at[me], norms.at[me], nsend.at[peer], nrecv.at[me],
            device_id=(peer, mine), device_id_type=MESH,
        ).start()
        sent.append(pltpu.make_async_remote_copy(
            norms.at[me], norms.at[peer], nsend.at[peer], nrecv.at[peer],
            device_id=(peer, mine), device_id_type=MESH,
        ))
    emit(2, cols3, v3_out).start()
    for copy in sent:
        copy.wait()
    v_sq = total(jnp.sum(norms[...], axis=0))
    h3 = mh2 - diag2 * h2 - off1 * h1
    off2 = jnp.sqrt(v_sq + total(h3 * h3))
    inv2 = 1.0 / off2
    alpha3 = off2 / beta3

    rho1 = jnp.sqrt(alpha1 * alpha1 + beta2 * beta2)
    cos1, sin1 = alpha1 / rho1, beta2 / rho1
    turn1, rhobar = sin1 * alpha2 / rho1, -cos1 * alpha2
    move1, phibar = cos1 * beta1 / rho1, sin1 * beta1
    rho2 = jnp.sqrt(rhobar * rhobar + beta3 * beta3)
    cos2, sin2 = rhobar / rho2, beta3 / rho2
    turn2, move2 = sin2 * alpha3 / rho2, cos2 * phibar / rho2

    walk = h2 - turn1 * h1
    tables[0] = move1 * h1 + move2 * walk
    tables[1] = inv2 * h3 - turn2 * walk
    kept = configs // n_inst
    xh_out[...] = tables[0, pl.ds(pl.multiple_of(mine * kept, kept), kept), pl.ds(0, samples)]
    wh_out[...] = tables[1, pl.ds(pl.multiple_of(mine * kept, kept), kept), pl.ds(0, samples)]

    mixes = [
        (move1 - move2 * turn1) * inv_p,
        move2 * inv1,
        turn2 * turn1 * inv_p,
        -turn2 * inv1,
        inv2,
    ]
    row = iota((8, 2 * F), 0)
    mix = jnp.zeros((8, 2 * F), f32)
    for index, value in enumerate(mixes):
        mix = jnp.where(row == index, value, mix)
    mix_out[...] = mix
    emit(0, cols1, v1_out).wait()
    emit(1, cols2, v2_out).wait()
    emit(2, cols3, v3_out).wait()


def combine(mix_ref, v1_ref, v2_ref, v3_ref, xh_ref, wh_ref, x_ref, w_ref, xt_ref, wt_ref):
    @pl.when(pl.program_id(0) == 0)
    def _():
        xt_ref[...] = xh_ref[...]
        wt_ref[...] = wh_ref[...]

    mix = [mix_ref[pl.ds(i, 1), pl.ds(0, 1)] for i in range(5)]
    used = pl.ds(0, x_ref.shape[0])
    v1, v2 = v1_ref[used, :], v2_ref[used, :]
    x_ref[...] = mix[0] * v1 + mix[1] * v2
    w_ref[...] = mix[2] * v1 + mix[3] * v2 + mix[4] * v3_ref[used, :]


def on_device(observed, basis, taps, epoch_owner, epoch_source, epoch_config, epoch_counts):
    n_src, n_inst = lax.axis_size("src"), lax.axis_size("inst")
    samples, epochs = observed.shape
    coefs = basis.shape[1]
    cap = max(2, epochs * 3 // (2 * n_src))
    rows = -(-cap // 16) * 8
    configs = KDEV * n_inst
    lo_n = 1
    while lo_n * lo_n * 4 <= n_src:
        lo_n *= 2
    hi_n = n_src // lo_n
    slots = 2 * rows * n_src * n_inst
    chunk = 512
    dims = (n_src, n_inst, rows, configs, hi_n, lo_n, chunk, SRC_DEV)
    vmem, smem = pl.BlockSpec(memory_space=pltpu.VMEM), pl.BlockSpec(memory_space=pltpu.SMEM)
    columns = jax.ShapeDtypeStruct((F, SRC_DEV), f32)
    v1, v2, v3, mix, xh, wh = pl.pallas_call(
        functools.partial(lanczos, dims),
        out_shape=(
            columns,
            columns,
            columns,
            jax.ShapeDtypeStruct((8, 2 * F), f32),
            jax.ShapeDtypeStruct((KDEV, samples), f32),
            jax.ShapeDtypeStruct((KDEV, samples), f32),
        ),
        in_specs=[vmem, vmem, smem, vmem, vmem, vmem, vmem],
        out_specs=(pl.BlockSpec(memory_space=pl.ANY),) * 3 + (vmem,) * 3,
        scratch_shapes=[
            pltpu.VMEM((n_src, rows, 2 * F), f32),
            pltpu.VMEM((n_inst, n_src, rows, 2 * F), f32),
            pltpu.VMEM((slots, F), f32),
            pltpu.VMEM((slots, 3 * F + configs), bf16),
            pltpu.VMEM((slots, F), f32),
            pltpu.VMEM((slots, F), f32),
            pltpu.VMEM((slots, configs), f32),
            pltpu.VMEM((F, F), f32),
            pltpu.VMEM((2, configs, F), f32),
            pltpu.VMEM((slots, 128), bf16),
            pltpu.VMEM((3 * F + configs, slots), bf16),
            pltpu.VMEM((F, SRC_DEV), f32),
            pltpu.VMEM((F, SRC_DEV), f32),
            pltpu.VMEM((F, SRC_DEV), f32),
            pltpu.VMEM((F, SRC_DEV), f32),
            pltpu.VMEM((F, SRC_DEV), f32),
            pltpu.VMEM((configs, SRC_DEV), f32),
            pltpu.SemaphoreType.DMA((3,)),
            pltpu.VMEM((hi_n, configs, 2 * F), f32),
            pltpu.VMEM((lo_n, configs, 2 * F), f32),
            pltpu.VMEM((hi_n, configs // 2, 2 * F), f32),
            pltpu.VMEM((lo_n, configs // 2, 2 * F), f32),
            pltpu.VMEM((n_src, 8, 2 * F), f32),
            pltpu.SemaphoreType.DMA((n_src,)),
            pltpu.SemaphoreType.DMA((n_src,)),
            pltpu.SemaphoreType.DMA((n_inst,)),
            pltpu.SemaphoreType.DMA((n_inst,)),
            pltpu.SemaphoreType.DMA((2, hi_n)),
            pltpu.SemaphoreType.DMA((2, hi_n)),
            pltpu.SemaphoreType.DMA((2, lo_n)),
            pltpu.SemaphoreType.DMA((2, lo_n)),
            pltpu.SemaphoreType.DMA((n_src,)),
            pltpu.SemaphoreType.DMA((n_src,)),
        ],
        compiler_params=pltpu.CompilerParams(
            collective_id=0, has_side_effects=True, vmem_limit_bytes=60 * 1024 * 1024
        ),
        name="lanczos",
    )(
        observed,
        basis.T,
        taps,
        epoch_owner.reshape(1, epochs),
        epoch_source.reshape(1, epochs),
        epoch_config.reshape(1, epochs),
        epoch_counts.reshape(1, 1),
    )
    block = SRC_DEV // 4
    whole = pl.BlockSpec((KDEV, samples), lambda i: (0, 0))
    part = pl.BlockSpec((F, block), lambda i: (0, i))
    kept = pl.BlockSpec((coefs, block), lambda i: (0, i))
    sol_c, walk_c, sol_h, walk_h = pl.pallas_call(
        combine,
        grid=(SRC_DEV // block,),
        out_shape=(jax.ShapeDtypeStruct((coefs, SRC_DEV), f32),) * 2
        + (jax.ShapeDtypeStruct((KDEV, samples), f32),) * 2,
        in_specs=[pl.BlockSpec((8, 2 * F), lambda i: (0, 0)), part, part, part, whole, whole],
        out_specs=(kept, kept, whole, whole),
        compiler_params=pltpu.CompilerParams(vmem_limit_bytes=60 * 1024 * 1024),
        name="combine",
    )(mix, v1, v2, v3, xh, wh)
    return (sol_c, sol_h.T, walk_c, walk_h.T)


def solution(mesh):
    placed = (
        P(None, ("src", "inst")),
        P(),
        P(),
        P(("src", "inst"), None),
        P(("src", "inst")),
        P(("src", "inst")),
        P(("src", "inst")),
    )
    return jax.shard_map(
        on_device,
        mesh=mesh,
        in_specs=placed,
        out_specs=(P(None, "src"), P(None, "inst"), P(None, "src"), P(None, "inst")),
        check_vma=False,
    )
```

profile of v0, /device:TPU:0, one launch (start us, length us, event | category | flops | bytes accessed | tf_op | source)
XLA Modules:
  0.0 51.1 jit_solution(14379243901673111336)
XLA Ops:
  1.3 45.8 %lanczos.1 = (f32[64,4096]{1,0:T(8,128)}, f32[64,4096]{1,0:T(8,128)}, f32[64,4096]{1,0:T(8,128)}, f32[8,128]{1,0:T(8,128)}, f32[16,60]{1,0:T(8,128)}, /*index=5*/f32[16,60]{1,0:T(8,128)}) custom-call(f32[60,512]{1,0:T(8,128)} %obs.1, f32[55,60]{1,0:T(8,128)} %bitcast.8, f32[9]{0:T(128)} %taps.1, s32[1,512]{1,0:T(1,128)} %bitcast.9, s32[1,512]{1,0:T(1,128)} %bitcast.10, ...), custom_call_target="tpu_custom_call" | custom-call | tf_op jit(solution)/shard_map/lanczos/pallas_call | solution.py:445
  47.1 4.0 %combine.1 = (f32[55,4096]{1,0:T(8,128)}, f32[55,4096]{1,0:T(8,128)}, f32[16,60]{1,0:T(8,128)}, f32[16,60]{1,0:T(8,128)}) custom-call(f32[8,128]{1,0:T(8,128)} %get-tuple-element.14.mix_ref, f32[64,4096]{1,0:T(8,128)} %get-tuple-element.15.v1_ref, f32[64,4096]{1,0:T(8,128)} %get-tuple-element.16.v2_ref, f32[64,4096]{1,0:T(8,128)} %get-tuple-element.17.v3_ref, ...), custom_call_target="tpu_custom_call" | custom-call | tf_op jit(solution)/shard_map/combine/pallas_call | solution.py:509
where the time goes:
time: 51.3 us; the launch traced here: 51.1 us
  Pallas kernels  49.8 us (97%)
  between operations  1.29 us (3%)
    pallas_call x1, Pallas kernels, on_device(): pl.pallas_call(functools.partial(lanczos, dims), out_shape=(columns, colu...  45.8 us
    pallas_call x1, Pallas kernels, on_device(): pl.pallas_call(combine, grid=(SRC_DEV // block,), out_shape=(jax.ShapeDty...  4 us

commit v1 on v0

--- a/solution.py
+++ b/solution.py
@@ -71,7 +71,7 @@
     obs, basis_t, taps, owner, source, config, counts,
     v1_out, v2_out, v3_out, mix_out, xh_out, wh_out,
     send, recv, slots, quads, c0s, cgs, nss, rpad, tables,
-    match, zt, cols1, cols2, cols3, grams, counts_c, named_c, out_sem,
+    match, cols1, cols2, cols3, grams, counts_c, named_c, out_sem,
     a1, a2, b1, b2, norms,
     send_sem, recv_sem, fsend_sem, frecv_sem, xsend, xrecv, ysend, yrecv, nsend, nrecv,
 ):
@@ -215,7 +215,7 @@
         0, steps, gather, (jnp.zeros((configs, 2 * F), f32), none, none), unroll=unroll
     )
 
-    lanes = match.shape[1]
+    lanes = match.shape[0]
     block = 512
 
     def here(at_block):
@@ -229,9 +229,9 @@
                 ).astype(bf16)
                 for i in range(block // lanes)
             ],
-            1,
+            0,
         )
-        got = jnp.dot(zt[...], hit, preferred_element_type=f32)
+        got = jnp.dot(hit, quads[...], preferred_element_type=f32).T
         c0 = got[:F] + got[F : 2 * F]
         cols1[here(at_block)] = c0
         counts_c[here(at_block)] = got[2 * F : 3 * F]
@@ -245,9 +245,8 @@
     blocks = sources // block
 
     def prepare_first():
-        name = slots[:, samples : samples + 1].astype(jnp.int32) - 1
-        match[...] = jnp.where((name & (lanes - 1)) == iota(match.shape, 1), name // lanes, -1).astype(f32).astype(bf16)
-        zt[...] = quads[...].astype(f32).T.astype(bf16)
+        name = id_row.astype(jnp.int32) - 1
+        match[...] = jnp.where((name & (lanes - 1)) == iota(match.shape, 0), name // lanes, -1).astype(f32).astype(bf16)
         lax.fori_loop(0, blocks // 4, deposit, 0)
 
     def finish_first():
@@ -464,8 +463,7 @@
             pltpu.VMEM((slots, configs), f32),
             pltpu.VMEM((F, F), f32),
             pltpu.VMEM((2, configs, F), f32),
-            pltpu.VMEM((slots, 128), bf16),
-            pltpu.VMEM((3 * F + configs, slots), bf16),
+            pltpu.VMEM((128, slots), bf16),
             pltpu.VMEM((F, SRC_DEV), f32),
             pltpu.VMEM((F, SRC_DEV), f32),
             pltpu.VMEM((F, SRC_DEV), f32),

time: 51.3 us -> 52 us (1.014)
  Pallas kernels: 49.8 us -> 50.5 us
    pallas_call x1, Pallas kernels: 45.8 us -> 46.5 us  [on_device(): pl.pallas_call(functools.partial(lanczos, dims), out_shape=(columns, colu...]
where the time goes in v1:
time: 52 us; the launch traced here: 51.7 us
  Pallas kernels  50.5 us (97%)
  between operations  1.29 us (2%)
    pallas_call x1, Pallas kernels, on_device(): pl.pallas_call(functools.partial(lanczos, dims), out_shape=(columns, colu...  46.5 us
    pallas_call x1, Pallas kernels, on_device(): pl.pallas_call(combine, grid=(SRC_DEV // block,), out_shape=(jax.ShapeDty...  4 us

profile of v1, /device:TPU:0, one launch (start us, length us, event | category | flops | bytes accessed | tf_op | source)
XLA Modules:
  0.0 51.7 jit_solution(12718821238799624181)
XLA Ops:
  1.3 46.5 %lanczos.1 = (f32[64,4096]{1,0:T(8,128)}, f32[64,4096]{1,0:T(8,128)}, f32[64,4096]{1,0:T(8,128)}, f32[8,128]{1,0:T(8,128)}, f32[16,60]{1,0:T(8,128)}, /*index=5*/f32[16,60]{1,0:T(8,128)}) custom-call(f32[60,512]{1,0:T(8,128)} %obs.1, f32[55,60]{1,0:T(8,128)} %bitcast.8, f32[9]{0:T(128)} %taps.1, s32[1,512]{1,0:T(1,128)} %bitcast.9, s32[1,512]{1,0:T(1,128)} %bitcast.10, ...), custom_call_target="tpu_custom_call" | custom-call | tf_op jit(solution)/shard_map/lanczos/pallas_call | solution.py:444
  47.7 4.0 %combine.1 = (f32[55,4096]{1,0:T(8,128)}, f32[55,4096]{1,0:T(8,128)}, f32[16,60]{1,0:T(8,128)}, f32[16,60]{1,0:T(8,128)}) custom-call(f32[8,128]{1,0:T(8,128)} %get-tuple-element.14.mix_ref, f32[64,4096]{1,0:T(8,128)} %get-tuple-element.15.v1_ref, f32[64,4096]{1,0:T(8,128)} %get-tuple-element.16.v2_ref, f32[64,4096]{1,0:T(8,128)} %get-tuple-element.17.v3_ref, ...), custom_call_target="tpu_custom_call" | custom-call | tf_op jit(solution)/shard_map/combine/pallas_call | solution.py:507
